TPU v7x, 128 devices: a whole 4x4x4 slice. The times are simulated.
128 devices in a mesh: pin: 32 (over z, x, core), board: 4 (over y).
Axes of the slice: x: 4, y: 4, z: 4, core: 2. Of those that a mesh axis runs over, the one named last changes fastest.
Arguments:
- features: bfloat16 [65536, 2048], P(('pin', 'board')), may hold values from -6 to 6
- w_message: bfloat16 [2048, 1024], replicated, may hold values from -0.125 to 0.125
- w_update: bfloat16 [1024, 1024], replicated, may hold values from -0.375 to 0.375
- cotangent: bfloat16 [65536, 1024], P(('pin', 'board')), may hold values from -6 to 6
- slot_pin: int32 [128, 128, 16], P(('pin', 'board')), may hold values from 0 to 511
- slot_board: int32 [128, 128, 16], P(('pin', 'board')), may hold values from 0 to 255
- slot_walk: int32 [128, 128, 16], P(('pin', 'board')), may hold values from 1 to 32, as said below
- pair_count: int32 [128, 128], P(('pin', 'board')), may hold values from 1 to 16, as said below
Outputs:
- output: bfloat16 [65536, 1024], P(('pin', 'board'))
- grad_message: bfloat16 [2048, 1024], replicated
- grad_update: bfloat16 [1024, 1024], replicated
Inputs may be any that keep to these rules, and one draw needn't show every extreme that they name: `slot_walk`: slots at or past their block's count hold arbitrary values in range. `pair_count`: in every draw some device receives 16 live slots from every device.
All inputs are finite; a program needn't handle non-finite values.
Results may differ from a plain program's by a relative error of at most 0.006.
The roundings to bfloat16 on the way count: a program that leaves them out, or rounds other values in their place, can miss the bound.
Values may be sent and summed in bfloat16 or wider, within the bound.
A program may use at most 128 MiB of HBM per device.

v0:
```python
import jax
import jax.numpy as jnp
from jax import lax
from jax.sharding import PartitionSpec as P


def silu_slope(value):
    sig = jax.nn.sigmoid(value)
    return sig * (1.0 + value * (1.0 - sig))


def body(features, w_message, w_update, cotangent, slot_pin, slot_board, slot_walk, pair_count):
    pin_count = lax.axis_size("pin")
    board_count = lax.axis_size("board")
    devices_all = pin_count * board_count
    slots = slot_pin.shape[2]
    pin_rows = features.shape[0]
    board_rows_dev = pin_rows // 2
    width = w_message.shape[1]
    slot_index = jnp.arange(slots, dtype=jnp.int32)
    is_live = slot_index[None, :] < pair_count[0][:, None]
    walks_int = jnp.where(is_live, slot_walk[0], 0)
    walks_flat = walks_int.reshape(-1).astype(jnp.float32)
    pins_flat = slot_pin[0].reshape(-1)
    pre_act = jnp.dot(features, w_message, preferred_element_type=jnp.float32)
    hidden = jax.nn.silu(pre_act).astype(jnp.bfloat16)
    messages = jnp.take(hidden, pins_flat, axis=0).reshape(devices_all, slots, width)
    boards_sent = slot_board[0]
    recv_messages, recv_boards, recv_walks = (
        lax.all_to_all(messages, ("pin", "board"), split_axis=0, concat_axis=0, tiled=True),
        lax.all_to_all(boards_sent, ("pin", "board"), split_axis=0, concat_axis=0, tiled=True),
        lax.all_to_all(walks_int, ("pin", "board"), split_axis=0, concat_axis=0, tiled=True),
    )
    recv_board_flat = recv_boards.reshape(-1)
    recv_weight = recv_walks.reshape(-1).astype(jnp.float32)
    board_match = jnp.arange(board_rows_dev, dtype=jnp.int32)[:, None] == recv_board_flat[None, :]
    board_weights = jnp.where(board_match, recv_weight[None, :], 0.0)
    board_degree = jnp.sum(board_weights, axis=1)
    board_total = jnp.dot(
        board_weights.astype(jnp.bfloat16),
        recv_messages.reshape(-1, width),
        preferred_element_type=jnp.float32,
    )
    board_rows = (board_total / jnp.maximum(board_degree, 1.0)[:, None]).astype(jnp.bfloat16)
    returned = jnp.take(board_rows, recv_board_flat, axis=0).reshape(devices_all, slots, width)
    read_rows = lax.all_to_all(returned, ("pin", "board"), split_axis=0, concat_axis=0, tiled=True)
    pin_match = jnp.arange(pin_rows, dtype=jnp.int32)[:, None] == pins_flat[None, :]
    pin_weights = jnp.where(pin_match, walks_flat[None, :], 0.0)
    pin_degree = jnp.sum(pin_weights, axis=1)
    neigh_total = jnp.dot(
        pin_weights.astype(jnp.bfloat16),
        read_rows.reshape(-1, width),
        preferred_element_type=jnp.float32,
    )
    neighbour = (neigh_total / jnp.maximum(pin_degree, 1.0)[:, None]).astype(jnp.bfloat16)
    update = jnp.dot(neighbour, w_update, preferred_element_type=jnp.float32)
    output = (hidden.astype(jnp.float32) + jax.nn.silu(update)).astype(jnp.bfloat16)
    d_update = (cotangent.astype(jnp.float32) * silu_slope(update)).astype(jnp.bfloat16)
    grad_update = lax.dot_general(
        neighbour, d_update, (((0,), (0,)), ((), ())), preferred_element_type=jnp.float32
    )
    d_neighbour = lax.dot_general(
        d_update, w_update, (((1,), (1,)), ((), ())), preferred_element_type=jnp.float32
    ).astype(jnp.bfloat16)
    slot_scale = walks_flat / jnp.maximum(jnp.take(pin_degree, pins_flat, axis=0), 1.0)
    slot_grad = (
        slot_scale[:, None] * jnp.take(d_neighbour, pins_flat, axis=0).astype(jnp.float32)
    ).astype(jnp.bfloat16)
    slot_grad = slot_grad.reshape(devices_all, slots, width)
    recv_grads = lax.all_to_all(
        slot_grad, ("pin", "board"), split_axis=0, concat_axis=0, tiled=True
    )
    board_sum = jnp.dot(
        board_match.astype(jnp.bfloat16),
        recv_grads.reshape(-1, width),
        preferred_element_type=jnp.float32,
    )
    board_grad = board_sum / jnp.maximum(board_degree, 1.0)[:, None]
    message_grad = (recv_weight[:, None] * jnp.take(board_grad, recv_board_flat, axis=0)).astype(
        jnp.bfloat16
    )
    message_grad = message_grad.reshape(devices_all, slots, width)
    back_grads = lax.all_to_all(
        message_grad, ("pin", "board"), split_axis=0, concat_axis=0, tiled=True
    )
    neigh_grad = jnp.dot(
        pin_match.astype(jnp.bfloat16),
        back_grads.reshape(-1, width),
        preferred_element_type=jnp.float32,
    )
    hidden_grad = cotangent.astype(jnp.float32) + neigh_grad
    d_pre = (hidden_grad * silu_slope(pre_act)).astype(jnp.bfloat16)
    grad_message = lax.dot_general(
        features, d_pre, (((0,), (0,)), ((), ())), preferred_element_type=jnp.float32
    )
    total_message, total_update = lax.psum((grad_message, grad_update), ("pin", "board"))
    return (output, total_message.astype(jnp.bfloat16), total_update.astype(jnp.bfloat16))


def solution(mesh):
    in_specs = (
        P(("pin", "board"), None),
        P(),
        P(),
        P(("pin", "board"), None),
        P(("pin", "board"), None, None),
        P(("pin", "board"), None, None),
        P(("pin", "board"), None, None),
        P(("pin", "board"), None),
    )
    out_specs = (P(("pin", "board"), None), P(), P())
    return jax.shard_map(body, mesh=mesh, in_specs=in_specs, out_specs=out_specs, check_vma=False)
```

profile of v0, /device:TPU:0, one launch (start us, length us, event | category | flops | bytes accessed | tf_op | source)
XLA Modules:
  0.0 491.2 jit_solution(6893740091082586250)
XLA Ops:
  0.6 0.0 copy-start
  0.6 0.9 copy.30
  1.6 1.5 compare_select_fusion
  3.1 11.1 %all-to-all-start.1 = ((s32[128,1,16]{2,1,0:T(1,128)}), s32[128,1,16]{2,1,0:T(1,128)S(1)}, u32[]{:S(2)}, u32[]{:S(2)}) async-start(s32[128,1,16]{2,1,0:T(1,128)} %compare_select_fusion), calls=%async_computation.1 | async-start | bytes 131072 | tf_op jit(solution)/shard_map/all_to_all | solution.py:32
  14.2 0.7 iota_compare_fusion.10
  15.0 0.8 copy.29
  15.8 0.1 eq.29
  15.8 0.1 reshape_squeeze.3
  15.9 0.1 squeeze.6
  16.0 0.1 lt.96
  16.2 0.5 select_reduce_fusion
  16.7 13.2 %gather_fusion.1 = f32[2048]{0:T(1024)S(1)} fusion(f32[512]{0:T(512)S(1)} %select_reduce_fusion, s32[2048]{0:T(1024)S(1)} %broadcast_clamp_fusion.1), kind=kCustom, calls=%fused_computation.3 | custom fusion | bytes 24576 | tf_op jit(solution)/shard_map/jit(_take)/gather | solution.py:65
  29.9 0.0 copy-done
  29.9 0.0 copy-start.6
  29.9 6.0 %multiply_convert_fusion.2 = (bf16[512,1024]{1,0:T(8,128)(2,1)S(1)}, f32[512,1024]{1,0:T(8,128)}) fusion(bf16[512,2048]{1,0:T(8,128)(2,1)S(1)} %copy-done, bf16[2048,1024]{1,0:T(8,128)(2,1)} %param.11), kind=kOutput, calls=%fused_computation.31 | convolution fusion | flops 2150105088 | bytes 9437184 | tf_op jit(solution)/shard_map/dot_general | solution.py:25
  35.9 0.0 copy-start.1
  35.9 0.0 copy-done.6
  35.9 0.8 copy.31
  36.8 9.6 %gather_fusion.3 = bf16[2048,1024]{1,0:T(8,128)(2,1)} fusion(bf16[512,1024]{1,0:T(8,128)(2,1)S(1)} %get-tuple-element.22, s32[2048]{0:T(1024)S(1)} %fusion.16), kind=kCustom, calls=%fused_computation.clone | custom fusion | bytes 8396800 | tf_op jit(solution)/shard_map/jit(_take)/gather | solution.py:27
  46.4 0.0 copy-done.1
  46.4 0.0 all-to-all-done.1
  46.4 9.8 %all-to-all-start = ((s32[128,1,16]{2,1,0:T(1,128)}), s32[128,1,16]{2,1,0:T(1,128)S(1)}, u32[]{:S(2)}, u32[]{:S(2)}) async-start(s32[128,1,16]{2,1,0:T(1,128)} %bitcast.1), calls=%async_computation | async-start | bytes 131072 | tf_op jit(solution)/shard_map/all_to_all | solution.py:31
  56.2 3.9 broadcast_select_fusion
  60.1 5.4 %all-to-all-done = s32[128,1,16]{2,1,0:T(1,128)S(1)} async-done(((s32[128,1,16]{2,1,0:T(1,128)}), s32[128,1,16]{2,1,0:T(1,128)S(1)}, u32[]{:S(2)}, u32[]{:S(2)}) %all-to-all-start) | async-done | bytes 8224 | tf_op jit(solution)/shard_map/all_to_all | solution.py:31
  65.5 5.8 %all-to-all-start.2 = ((bf16[128,16,1024]{2,1,0:T(8,128)(2,1)}), bf16[128,16,1024]{2,1,0:T(8,128)(2,1)}, u32[]{:S(2)}, u32[]{:S(2)}) async-start(bf16[128,16,1024]{2,1,0:T(8,128)(2,1)} %bitcast.33), calls=%async_computation.2 | async-start | bytes 8388608 | tf_op jit(solution)/shard_map/all_to_all | solution.py:30
  71.3 0.2 convert_reduce_fusion
  71.5 0.1 convert_element_type.85
  71.6 0.1 reshape.255
  71.7 0.6 broadcast.161
  72.3 0.8 reduce.9
  73.1 0.1 reshape.252
  73.2 0.3 select_reduce_fusion.1
  73.5 49.3 %all-to-all-done.2 = bf16[128,16,1024]{2,1,0:T(8,128)(2,1)} async-done(((bf16[128,16,1024]{2,1,0:T(8,128)(2,1)}), bf16[128,16,1024]{2,1,0:T(8,128)(2,1)}, u32[]{:S(2)}, u32[]{:S(2)}) %all-to-all-start.2) | async-done | bytes 4194336 | tf_op jit(solution)/shard_map/all_to_all | solution.py:30
  122.8 3.4 fusion.10
  126.3 9.6 %gather_fusion = bf16[2048,1024]{1,0:T(8,128)(2,1)} fusion(bf16[256,1024]{1,0:T(8,128)(2,1)S(1)} %fusion.10, s32[2048]{0:T(1024)S(1)} %broadcast_clamp_fusion), kind=kCustom, calls=%fused_computation.2 | custom fusion | bytes 8396800 | tf_op jit(solution)/shard_map/jit(_take)/gather | solution.py:45
  135.9 3.9 broadcast_select_fusion.1
  139.7 6.0 %all-to-all-start.3 = ((bf16[128,16,1024]{2,1,0:T(8,128)(2,1)}), bf16[128,16,1024]{2,1,0:T(8,128)(2,1)}, u32[]{:S(2)}, u32[]{:S(2)}) async-start(bf16[128,16,1024]{2,1,0:T(8,128)(2,1)} %broadcast_select_fusion.1), calls=%async_computation.3 | async-start | bytes 8388608 | tf_op jit(solution)/shard_map/all_to_all | solution.py:46
  145.8 51.3 %all-to-all-done.3 = bf16[128,16,1024]{2,1,0:T(8,128)(2,1)} async-done(((bf16[128,16,1024]{2,1,0:T(8,128)(2,1)}), bf16[128,16,1024]{2,1,0:T(8,128)(2,1)}, u32[]{:S(2)}, u32[]{:S(2)}) %all-to-all-start.3) | async-done | bytes 4194336 | tf_op jit(solution)/shard_map/all_to_all | solution.py:46
  197.1 0.0 copy-start.2
  197.1 0.0 copy-start.7
  197.1 0.0 copy-start.8
  197.1 4.7 divide_convert_fusion
  201.8 0.0 copy-done.2
  201.8 0.0 copy-done.7
  201.8 0.0 copy-done.8
  201.8 0.0 copy-start.3
  201.8 3.1 fusion.1
  204.9 0.0 copy-done.3
  204.9 1.0 copy-done.5
  205.9 1.3 convolution_convert_fusion
  207.2 9.6 %gather_fusion.4 = bf16[2048,1024]{1,0:T(8,128)(2,1)} fusion(bf16[512,1024]{1,0:T(8,128)(2,1)S(1)} %convolution_convert_fusion, s32[2048]{0:T(1024)S(1)} %fusion.16), kind=kCustom, calls=%fused_computation.1.clone | custom fusion | bytes 8396800 | tf_op jit(solution)/shard_map/jit(_take)/gather | solution.py:67
  216.8 4.2 multiply_convert_fusion.1
  221.0 5.8 %all-to-all-start.4 = ((bf16[128,16,1024]{2,1,0:T(8,128)(2,1)}), bf16[128,16,1024]{2,1,0:T(8,128)(2,1)}, u32[]{:S(2)}, u32[]{:S(2)}) async-start(bf16[128,16,1024]{2,1,0:T(8,128)(2,1)} %bitcast.34), calls=%async_computation.4 | async-start | bytes 8388608 | tf_op jit(solution)/shard_map/all_to_all | solution.py:70
  226.9 51.5 %all-to-all-done.4 = bf16[128,16,1024]{2,1,0:T(8,128)(2,1)} async-done(((bf16[128,16,1024]{2,1,0:T(8,128)(2,1)}), bf16[128,16,1024]{2,1,0:T(8,128)(2,1)}, u32[]{:S(2)}, u32[]{:S(2)}) %all-to-all-start.4) | async-done | bytes 4194336 | tf_op jit(solution)/shard_map/all_to_all | solution.py:70
  278.3 3.4 fusion.11
  281.8 9.9 %gather_fusion.2 = f32[2048,1024]{1,0:T(8,128)} fusion(f32[256,1024]{1,0:T(8,128)S(1)} %fusion.11, s32[2048]{0:T(1024)S(1)} %broadcast_clamp_fusion), kind=kCustom, calls=%fused_computation.4 | custom fusion | bytes 16785408 | tf_op jit(solution)/shard_map/jit(_take)/gather | solution.py:79
  291.7 5.3 %multiply_convert_fusion = bf16[128,16,1024]{2,1,0:T(8,128)(2,1)} fusion(f32[128,16,1024]{2,1,0:T(8,128)} %bitcast.31, f32[128,16]{1,0:T(8,128)S(1)} %bitcast.38, pred[128,16]{1,0:T(8,128)(4,1)S(1)} %compare_and_fusion), kind=kLoop, calls=%fused_computation.5 | loop fusion | flops 6291456 | bytes 12593152 | tf_op jit(solution)/shard_map/convert_element_type | solution.py:79
  296.9 6.2 %all-to-all-start.5 = ((bf16[128,16,1024]{2,1,0:T(8,128)(2,1)}), bf16[128,16,1024]{2,1,0:T(8,128)(2,1)}, u32[]{:S(2)}, u32[]{:S(2)}) async-start(bf16[128,16,1024]{2,1,0:T(8,128)(2,1)} %multiply_convert_fusion), calls=%async_computation.5 | async-start | bytes 8388608 | tf_op jit(solution)/shard_map/all_to_all | solution.py:83
  303.1 0.0 copy-done.4
  303.1 4.4 fusion.20
  307.6 46.8 %all-to-all-done.5 = bf16[128,16,1024]{2,1,0:T(8,128)(2,1)} async-done(((bf16[128,16,1024]{2,1,0:T(8,128)(2,1)}), bf16[128,16,1024]{2,1,0:T(8,128)(2,1)}, u32[]{:S(2)}, u32[]{:S(2)}) %all-to-all-start.5) | async-done | bytes 4194336 | tf_op jit(solution)/shard_map/all_to_all | solution.py:83
  354.4 11.1 %convolution_bitcast_fusion = f32[2048,1024]{0,1:T(8,128)} fusion(bf16[512,2048]{1,0:T(8,128)(2,1)S(1)} %copy-done, bf16[512,1024]{1,0:T(8,128)(2,1)} %param.13, f32[512,1024]{1,0:T(8,128)} %get-tuple-element.23, bf16[2048,1024]{1,0:T(8,128)(2,1)} %bitcast.14, s32[2048]{0:T(1024)S(1)} %eq.29), kind=kOutput, calls=%fused_computation.9 | convolution fusion | flops 4301783040 | bytes 17833984 | tf_op jit(solution)/shard_map/dot_general | solution.py:93
  365.6 119.3 %all-reduce.2 = (bf16[2048,1024]{0,1:T(8,128)(2,1)}, bf16[1024,1024]{1,0:T(8,128)(2,1)}) all-reduce(f32[2048,1024]{0,1:T(8,128)} %convolution_bitcast_fusion, f32[1024,1024]{1,0:T(8,128)} %fusion.20), channel_id=1, replica_groups=mesh['pin'=32,'board'=4] {'pin','board'}, use_global_device_ids=true, to_apply=%region_2.4 | all-reduce | flops 3145728 | bytes 18874368 | tf_op jit(solution)/shard_map/psum | solution.py:96
  484.8 6.4 %copy.34 = bf16[2048,1024]{1,0:T(8,128)(2,1)} copy(bf16[2048,1024]{0,1:T(8,128)(2,1)} %get-tuple-element.16) | data formatting | bytes 8388608
  (13 shorter events, 0.1 us)
Async XLA Ops:
  0.6 29.3 %copy-start = (bf16[512,2048]{1,0:T(8,128)(2,1)S(1)}, bf16[512,2048]{1,0:T(8,128)(2,1)}, u32[]{:S(2)}) copy-start(bf16[512,2048]{1,0:T(8,128)(2,1)} %param.10) | copy-start | bytes 6291460
  3.1 43.3 %all-to-all-start.1 = ((s32[128,1,16]{2,1,0:T(1,128)}), s32[128,1,16]{2,1,0:T(1,128)S(1)}, u32[]{:S(2)}, u32[]{:S(2)}) async-start(s32[128,1,16]{2,1,0:T(1,128)} %compare_select_fusion), calls=%async_computation.1 | async-start | bytes 131072 | tf_op jit(solution)/shard_map/all_to_all | solution.py:32
  29.9 6.0 %copy-start.6 = (s32[1,128,16]{1,2,0:T(8,128)S(1)}, s32[1,128,16]{1,2,0:T(8,128)}, u32[]{:S(2)}) copy-start(s32[1,128,16]{1,2,0:T(8,128)} %param.15) | copy-start | bytes 24580
  35.9 10.5 %copy-start.1 = (bf16[512,1024]{1,0:T(8,128)(2,1)}, bf16[512,1024]{1,0:T(8,128)(2,1)S(1)}, u32[]{:S(2)}) copy-start(bf16[512,1024]{1,0:T(8,128)(2,1)S(1)} %get-tuple-element.22) | copy-start | bytes 3145732
  46.4 19.1 %all-to-all-start = ((s32[128,1,16]{2,1,0:T(1,128)}), s32[128,1,16]{2,1,0:T(1,128)S(1)}, u32[]{:S(2)}, u32[]{:S(2)}) async-start(s32[128,1,16]{2,1,0:T(1,128)} %bitcast.1), calls=%async_computation | async-start | bytes 131072 | tf_op jit(solution)/shard_map/all_to_all | solution.py:31
  65.5 57.4 %all-to-all-start.2 = ((bf16[128,16,1024]{2,1,0:T(8,128)(2,1)}), bf16[128,16,1024]{2,1,0:T(8,128)(2,1)}, u32[]{:S(2)}, u32[]{:S(2)}) async-start(bf16[128,16,1024]{2,1,0:T(8,128)(2,1)} %bitcast.33), calls=%async_computation.2 | async-start | bytes 8388608 | tf_op jit(solution)/shard_map/all_to_all | solution.py:30
  139.7 57.4 %all-to-all-start.3 = ((bf16[128,16,1024]{2,1,0:T(8,128)(2,1)}), bf16[128,16,1024]{2,1,0:T(8,128)(2,1)}, u32[]{:S(2)}, u32[]{:S(2)}) async-start(bf16[128,16,1024]{2,1,0:T(8,128)(2,1)} %broadcast_select_fusion.1), calls=%async_computation.3 | async-start | bytes 8388608 | tf_op jit(solution)/shard_map/all_to_all | solution.py:46
  197.1 4.7 copy-start.2
  197.1 4.7 copy-start.7
  197.1 4.7 copy-start.8
  201.8 3.1 copy-start.3
  204.9 1.0 copy-start.5
  221.0 57.4 %all-to-all-start.4 = ((bf16[128,16,1024]{2,1,0:T(8,128)(2,1)}), bf16[128,16,1024]{2,1,0:T(8,128)(2,1)}, u32[]{:S(2)}, u32[]{:S(2)}) async-start(bf16[128,16,1024]{2,1,0:T(8,128)(2,1)} %bitcast.34), calls=%async_computation.4 | async-start | bytes 8388608 | tf_op jit(solution)/shard_map/all_to_all | solution.py:70
  296.9 6.2 %copy-start.4 = (bf16[512,1024]{1,0:T(8,128)(2,1)S(1)}, bf16[512,1024]{1,0:T(8,128)(2,1)}, u32[]{:S(2)}) copy-start(bf16[512,1024]{1,0:T(8,128)(2,1)} %copy-done.3) | copy-start | bytes 3145732
  296.9 57.5 %all-to-all-start.5 = ((bf16[128,16,1024]{2,1,0:T(8,128)(2,1)}), bf16[128,16,1024]{2,1,0:T(8,128)(2,1)}, u32[]{:S(2)}, u32[]{:S(2)}) async-start(bf16[128,16,1024]{2,1,0:T(8,128)(2,1)} %multiply_convert_fusion), calls=%async_computation.5 | async-start | bytes 8388608 | tf_op jit(solution)/shard_map/all_to_all | solution.py:83
where the time goes:
time: 492 us; the launch traced here: 491 us
  waiting for transfers between devices  204 us (41%)
  blocking collectives  119 us (24%)
  local copies, waits for them, and re-layouts  63.1 us (13%)
  starting transfers between devices  44.8 us (9%)
  matrix products  37.5 us (8%)
  other arithmetic  21.3 us (4%)
    psum x1, blocking collectives, body(): lax.psum((grad_message, grad_update), ('pin', 'board'))  119 us
    all_to_all x1, waiting for transfers between devices, body(): lax.all_to_all(slot_grad, ('pin', 'board'), split_axis=0, concat_axis=0,...  51.5 us
    all_to_all x1, waiting for transfers between devices, body(): lax.all_to_all(returned, ('pin', 'board'), split_axis=0, concat_axis=0, t...  51.3 us
    all_to_all x1, waiting for transfers between devices, body(): lax.all_to_all(messages, ('pin', 'board'), split_axis=0, concat_axis=0, t...  49.3 us
    all_to_all x1, waiting for transfers between devices, body(): lax.all_to_all(message_grad, ('pin', 'board'), split_axis=0, concat_axis=...  46.8 us
    gather x1, local copies, waits for them, and re-layouts, body(): jnp.take(pin_degree, pins_flat, axis=0)  13.2 us
    dot_general x1, matrix products, body(): lax.dot_general(features, d_pre, (((0,), (0,)), ((), ())), preferred_elem...  11.1 us
    all_to_all x1, starting transfers between devices, body(): lax.all_to_all(walks_int, ('pin', 'board'), split_axis=0, concat_axis=0,...  11.1 us
  transfers between devices with their start and end apart: 6, of which 5 were waited for; matrix products, arithmetic and copies ran while one was open for 9% of the time, Pallas kernels for 0%

commit v1 on v0

--- a/solution.py
+++ b/solution.py
@@ -93,7 +93,7 @@
     grad_message = lax.dot_general(
         features, d_pre, (((0,), (0,)), ((), ())), preferred_element_type=jnp.float32
     )
-    total_message, total_update = lax.psum((grad_message, grad_update), ("pin", "board"))
+    total_message, total_update = lax.psum(lax.psum((grad_message, grad_update), "board"), "pin")
     return (output, total_message.astype(jnp.bfloat16), total_update.astype(jnp.bfloat16))
 
 

time: 492 us -> 793 us (1.61)
  waiting for transfers between devices: 204 us -> 429 us
  blocking collectives: 119 us -> 182 us
  between operations: 0.91 us -> 14.3 us
    psum x0 -> x1, waiting for transfers between devices: none -> 225 us  [body(): lax.psum((grad_message, grad_update), 'board')]
    psum x1, blocking collectives: 119 us -> 182 us  [body(): lax.psum(lax.psum((grad_message, grad_update), 'board'), 'pin')]
  transfers between devices with their start and end apart: 6 -> 7, of which waited for: 5 -> 6; matrix products, arithmetic and copies ran while one was open for 9% -> 5% of each run, Pallas kernels for 0% -> 0%
where the time goes in v1:
time: 793 us
  waiting for transfers between devices  429 us (54%)
  blocking collectives  182 us (23%)
  local copies, waits for them, and re-layouts  63.2 us (8%)
  starting transfers between devices  44.8 us (6%)
  matrix products  37.6 us (5%)
  other arithmetic  21.4 us (3%)
  between operations  14.3 us (2%)
    psum x1, waiting for transfers between devices, body(): lax.psum((grad_message, grad_update), 'board')  225 us
    psum x1, blocking collectives, body(): lax.psum(lax.psum((grad_message, grad_update), 'board'), 'pin')  182 us
    all_to_all x1, waiting for transfers between devices, body(): lax.all_to_all(slot_grad, ('pin', 'board'), split_axis=0, concat_axis=0,...  51.5 us
    all_to_all x1, waiting for transfers between devices, body(): lax.all_to_all(returned, ('pin', 'board'), split_axis=0, concat_axis=0, t...  51.3 us
    all_to_all x1, waiting for transfers between devices, body(): lax.all_to_all(messages, ('pin', 'board'), split_axis=0, concat_axis=0, t...  49.2 us
    all_to_all x1, waiting for transfers between devices, body(): lax.all_to_all(message_grad, ('pin', 'board'), split_axis=0, concat_axis=...  46.8 us
  transfers between devices with their start and end apart: 7, of which 6 were waited for; matrix products, arithmetic and copies ran while one was open for 5% of the time, Pallas kernels for 0%

profile of v1, /device:TPU:0, one launch (start us, length us, event | category | flops | bytes accessed | tf_op | source)
XLA Modules:
  0.0 792.6 jit_solution(14862038358802426396)
XLA Ops:
  7.2 0.0 copy-start
  7.2 0.9 copy.30
  8.1 1.5 compare_select_fusion
  9.6 11.1 %all-to-all-start.1 = ((s32[128,1,16]{2,1,0:T(1,128)}), s32[128,1,16]{2,1,0:T(1,128)S(1)}, u32[]{:S(2)}, u32[]{:S(2)}) async-start(s32[128,1,16]{2,1,0:T(1,128)} %compare_select_fusion), calls=%async_computation.1 | async-start | bytes 131072 | tf_op jit(solution)/shard_map/all_to_all | solution.py:32
  20.8 0.7 iota_compare_fusion.10
  21.5 0.8 copy.29
  22.3 0.1 eq.29
  22.4 0.1 reshape_squeeze.3
  22.5 0.1 squeeze.6
  22.6 0.1 lt.96
  22.7 0.5 select_reduce_fusion
  23.2 13.2 %gather_fusion.1 = f32[2048]{0:T(1024)S(1)} fusion(f32[512]{0:T(512)S(1)} %select_reduce_fusion, s32[2048]{0:T(1024)S(1)} %broadcast_clamp_fusion.1), kind=kCustom, calls=%fused_computation.3 | custom fusion | bytes 24576 | tf_op jit(solution)/shard_map/jit(_take)/gather | solution.py:65
  36.4 0.0 copy-done
  36.5 0.0 copy-start.6
  36.5 6.0 multiply_convert_fusion.2
  42.5 0.0 copy-start.1
  42.5 0.0 copy-done.6
  42.5 0.9 copy.31
  43.4 9.6 %gather_fusion.3 = bf16[2048,1024]{1,0:T(8,128)(2,1)} fusion(bf16[512,1024]{1,0:T(8,128)(2,1)S(1)} %get-tuple-element.24, s32[2048]{0:T(1024)S(1)} %fusion.16), kind=kCustom, calls=%fused_computation.clone | custom fusion | bytes 8396800 | tf_op jit(solution)/shard_map/jit(_take)/gather | solution.py:27
  53.0 0.0 copy-done.1
  53.0 0.0 all-to-all-done.1
  53.0 9.8 %all-to-all-start = ((s32[128,1,16]{2,1,0:T(1,128)}), s32[128,1,16]{2,1,0:T(1,128)S(1)}, u32[]{:S(2)}, u32[]{:S(2)}) async-start(s32[128,1,16]{2,1,0:T(1,128)} %bitcast.1), calls=%async_computation | async-start | bytes 131072 | tf_op jit(solution)/shard_map/all_to_all | solution.py:31
  62.7 3.9 broadcast_select_fusion
  66.6 5.4 all-to-all-done
  72.0 5.8 all-to-all-start.2
  77.9 0.2 convert_reduce_fusion
  78.1 0.1 convert_element_type.85
  78.2 0.1 reshape.255
  78.3 0.6 broadcast.161
  78.9 0.8 reduce.9
  79.7 0.1 reshape.252
  79.8 0.3 select_reduce_fusion.1
  80.2 49.2 %all-to-all-done.2 = bf16[128,16,1024]{2,1,0:T(8,128)(2,1)} async-done(((bf16[128,16,1024]{2,1,0:T(8,128)(2,1)}), bf16[128,16,1024]{2,1,0:T(8,128)(2,1)}, u32[]{:S(2)}, u32[]{:S(2)}) %all-to-all-start.2) | async-done | bytes 4194336 | tf_op jit(solution)/shard_map/all_to_all | solution.py:30
  129.4 3.4 fusion.10
  132.8 9.6 %gather_fusion = bf16[2048,1024]{1,0:T(8,128)(2,1)} fusion(bf16[256,1024]{1,0:T(8,128)(2,1)S(1)} %fusion.10, s32[2048]{0:T(1024)S(1)} %broadcast_clamp_fusion), kind=kCustom, calls=%fused_computation.2 | custom fusion | bytes 8396800 | tf_op jit(solution)/shard_map/jit(_take)/gather | solution.py:45
  142.5 3.9 broadcast_select_fusion.1
  146.3 6.0 all-to-all-start.3
  152.4 51.3 %all-to-all-done.3 = bf16[128,16,1024]{2,1,0:T(8,128)(2,1)} async-done(((bf16[128,16,1024]{2,1,0:T(8,128)(2,1)}), bf16[128,16,1024]{2,1,0:T(8,128)(2,1)}, u32[]{:S(2)}, u32[]{:S(2)}) %all-to-all-start.3) | async-done | bytes 4194336 | tf_op jit(solution)/shard_map/all_to_all | solution.py:46
  203.7 4.7 divide_convert_fusion
  208.4 0.0 copy-done.2
  208.4 0.0 copy-done.7
  208.4 0.0 copy-done.8
  208.4 0.0 copy-start.3
  208.4 3.1 fusion.1
  211.5 0.0 copy-done.3
  211.5 1.1 copy-done.5
  212.6 1.3 convolution_convert_fusion
  213.9 9.6 %gather_fusion.4 = bf16[2048,1024]{1,0:T(8,128)(2,1)} fusion(bf16[512,1024]{1,0:T(8,128)(2,1)S(1)} %convolution_convert_fusion, s32[2048]{0:T(1024)S(1)} %fusion.16), kind=kCustom, calls=%fused_computation.1.clone | custom fusion | bytes 8396800 | tf_op jit(solution)/shard_map/jit(_take)/gather | solution.py:67
  223.5 4.2 multiply_convert_fusion.1
  227.6 5.8 all-to-all-start.4
  233.5 51.5 %all-to-all-done.4 = bf16[128,16,1024]{2,1,0:T(8,128)(2,1)} async-done(((bf16[128,16,1024]{2,1,0:T(8,128)(2,1)}), bf16[128,16,1024]{2,1,0:T(8,128)(2,1)}, u32[]{:S(2)}, u32[]{:S(2)}) %all-to-all-start.4) | async-done | bytes 4194336 | tf_op jit(solution)/shard_map/all_to_all | solution.py:70
  285.0 3.4 fusion.11
  288.4 9.9 %gather_fusion.2 = f32[2048,1024]{1,0:T(8,128)} fusion(f32[256,1024]{1,0:T(8,128)S(1)} %fusion.11, s32[2048]{0:T(1024)S(1)} %broadcast_clamp_fusion), kind=kCustom, calls=%fused_computation.4 | custom fusion | bytes 16785408 | tf_op jit(solution)/shard_map/jit(_take)/gather | solution.py:79
  298.3 5.3 multiply_convert_fusion
  303.6 6.0 all-to-all-start.5
  309.5 0.3 all-reduce.5.cloned.1.call-start
  309.8 0.0 copy-done.4
  309.8 4.5 fusion.20
  314.3 46.8 %all-to-all-done.5 = bf16[128,16,1024]{2,1,0:T(8,128)(2,1)} async-done(((bf16[128,16,1024]{2,1,0:T(8,128)(2,1)}), bf16[128,16,1024]{2,1,0:T(8,128)(2,1)}, u32[]{:S(2)}, u32[]{:S(2)}) %all-to-all-start.5) | async-done | bytes 4194336 | tf_op jit(solution)/shard_map/all_to_all | solution.py:83
  361.1 11.2 %convolution_bitcast_fusion = f32[2048,1024]{0,1:T(8,128)} fusion(bf16[512,2048]{1,0:T(8,128)(2,1)S(1)} %copy-done, bf16[512,1024]{1,0:T(8,128)(2,1)} %param.13, f32[512,1024]{1,0:T(8,128)} %get-tuple-element.25, bf16[2048,1024]{1,0:T(8,128)(2,1)} %bitcast.14, s32[2048]{0:T(1024)S(1)} %eq.29), kind=kOutput, calls=%fused_computation.9 | convolution fusion | flops 4301783040 | bytes 17833984 | tf_op jit(solution)/shard_map/dot_general | solution.py:93
  372.2 0.0 all-reduce.5.cloned.1.call-update
  372.2 224.8 %all-reduce.5.cloned.1.call-done = (f32[2048,1024]{0,1:T(8,128)}, f32[1024,1024]{1,0:T(8,128)}) async-done(((f32[2048,1024]{0,1:T(8,128)}, f32[1024,1024]{1,0:T(8,128)}), (f32[2048,1024]{0,1:T(8,128)}, f32[1024,1024]{1,0:T(8,128)})) %all-reduce.5.cloned.1.call-update) | async-done | bytes 12582928 | tf_op jit(solution)/shard_map/psum | solution.py:96
  597.1 182.3 %all-reduce.6 = (bf16[2048,1024]{0,1:T(8,128)(2,1)}, bf16[1024,1024]{1,0:T(8,128)(2,1)}) all-reduce(f32[2048,1024]{0,1:T(8,128)} %get-tuple-element.18, f32[1024,1024]{1,0:T(8,128)} %get-tuple-element.19), channel_id=1, replica_groups=mesh['pin'=32,'board'=4] {'pin'}, use_global_device_ids=true, to_apply=%region_3.5 | all-reduce | flops 3145728 | bytes 18874368 | tf_op jit(solution)/shard_map/psum | solution.py:96
  779.4 6.4 copy.34
  (16 shorter events, 0.1 us)
Async XLA Ops:
  7.2 29.3 %copy-start = (bf16[512,2048]{1,0:T(8,128)(2,1)S(1)}, bf16[512,2048]{1,0:T(8,128)(2,1)}, u32[]{:S(2)}) copy-start(bf16[512,2048]{1,0:T(8,128)(2,1)} %param.10) | copy-start | bytes 6291460
  9.6 43.4 %all-to-all-start.1 = ((s32[128,1,16]{2,1,0:T(1,128)}), s32[128,1,16]{2,1,0:T(1,128)S(1)}, u32[]{:S(2)}, u32[]{:S(2)}) async-start(s32[128,1,16]{2,1,0:T(1,128)} %compare_select_fusion), calls=%async_computation.1 | async-start | bytes 131072 | tf_op jit(solution)/shard_map/all_to_all | solution.py:32
  36.5 6.0 copy-start.6
  42.5 10.5 %copy-start.1 = (bf16[512,1024]{1,0:T(8,128)(2,1)}, bf16[512,1024]{1,0:T(8,128)(2,1)S(1)}, u32[]{:S(2)}) copy-start(bf16[512,1024]{1,0:T(8,128)(2,1)S(1)} %get-tuple-element.24) | copy-start | bytes 3145732
  53.0 19.1 %all-to-all-start = ((s32[128,1,16]{2,1,0:T(1,128)}), s32[128,1,16]{2,1,0:T(1,128)S(1)}, u32[]{:S(2)}, u32[]{:S(2)}) async-start(s32[128,1,16]{2,1,0:T(1,128)} %bitcast.1), calls=%async_computation | async-start | bytes 131072 | tf_op jit(solution)/shard_map/all_to_all | solution.py:31
  72.0 57.4 %all-to-all-start.2 = ((bf16[128,16,1024]{2,1,0:T(8,128)(2,1)}), bf16[128,16,1024]{2,1,0:T(8,128)(2,1)}, u32[]{:S(2)}, u32[]{:S(2)}) async-start(bf16[128,16,1024]{2,1,0:T(8,128)(2,1)} %bitcast.33), calls=%async_computation.2 | async-start | bytes 8388608 | tf_op jit(solution)/shard_map/all_to_all | solution.py:30
  146.3 57.4 %all-to-all-start.3 = ((bf16[128,16,1024]{2,1,0:T(8,128)(2,1)}), bf16[128,16,1024]{2,1,0:T(8,128)(2,1)}, u32[]{:S(2)}, u32[]{:S(2)}) async-start(bf16[128,16,1024]{2,1,0:T(8,128)(2,1)} %broadcast_select_fusion.1), calls=%async_computation.3 | async-start | bytes 8388608 | tf_op jit(solution)/shard_map/all_to_all | solution.py:46
  203.7 4.7 copy-start.2
  203.7 4.7 copy-start.7
  203.7 4.7 copy-start.8
  208.4 3.1 copy-start.3
  211.5 1.1 copy-start.5
  227.6 57.4 %all-to-all-start.4 = ((bf16[128,16,1024]{2,1,0:T(8,128)(2,1)}), bf16[128,16,1024]{2,1,0:T(8,128)(2,1)}, u32[]{:S(2)}, u32[]{:S(2)}) async-start(bf16[128,16,1024]{2,1,0:T(8,128)(2,1)} %bitcast.34), calls=%async_computation.4 | async-start | bytes 8388608 | tf_op jit(solution)/shard_map/all_to_all | solution.py:70
  303.6 6.3 copy-start.4
  303.6 57.5 %all-to-all-start.5 = ((bf16[128,16,1024]{2,1,0:T(8,128)(2,1)}), bf16[128,16,1024]{2,1,0:T(8,128)(2,1)}, u32[]{:S(2)}, u32[]{:S(2)}) async-start(bf16[128,16,1024]{2,1,0:T(8,128)(2,1)} %multiply_convert_fusion), calls=%async_computation.5 | async-start | bytes 8388608 | tf_op jit(solution)/shard_map/all_to_all | solution.py:83
  309.5 287.5 %all-reduce.5.cloned.1.call-start = ((), (), s32[]{:S(2)}) async-start(), calls=%async_computation.6 | async-start | bytes 25165824 | tf_op jit(solution)/shard_map/psum | solution.py:96
Sparse Core Ops, SparseCore 0:
  372.4 224.6 all-reduce.4
